TPU v7x, 32 devices: a whole 2x2x4 slice. The times are simulated.
32 devices in a mesh: freq: 2 (over x), tm: 8 (over z, core), batch: 2 (over y).
Axes of the slice: x: 2, y: 2, z: 4, core: 2. Of those that a mesh axis runs over, the one named last changes fastest.
Arguments:
- patches: bfloat16 [16, 8, 256, 384], P('batch', 'freq', 'tm'), may hold values from -6 to 6
- patch_mask: int32 [16, 8, 256], P('batch', 'freq', 'tm'), may hold values 0 or 1
- clip_lengths: int32 [16], P('batch'), may hold values from 1 to 256
- target_index: int32 [16, 8, 256], P('batch', 'freq', 'tm'), may hold values from 0 to 127
- targets: bfloat16 [16, 128, 384], P('batch'), may hold values from -0.41992188 to 0.41992188
- out_grad: bfloat16 [16, 8, 256, 384], P('batch', 'freq', 'tm'), may hold values from -6 to 6
- mask_embed: bfloat16 [384], replicated, may hold values from -4 to 4
- ln1_gain: bfloat16 [384], replicated, may hold values from 0.25 to 1.75
- ln1_shift: bfloat16 [384], replicated, may hold values from -1.5 to 1.5
- w_qkv: bfloat16 [384, 1152], replicated, may hold values from -0.3125 to 0.3125
- bias_q: bfloat16 [384], replicated, may hold values from -1.5 to 1.5
- bias_v: bfloat16 [384], replicated, may hold values from -0.25 to 0.25
- w_out: bfloat16 [384, 384], replicated, may hold values from -1.5 to 1.5
- bias_out: bfloat16 [384], replicated, may hold values from -1.5 to 1.5
- ln2_gain: bfloat16 [384], replicated, may hold values from 0.25 to 1.75
- ln2_shift: bfloat16 [384], replicated, may hold values from -1.5 to 1.5
- w_up: bfloat16 [384, 1536], replicated, may hold values from -0.3125 to 0.3125
- bias_up: bfloat16 [1536], replicated, may hold values from -1.5 to 1.5
- w_down: bfloat16 [1536, 384], replicated, may hold values from -0.15625 to 0.15625
- bias_down: bfloat16 [384], replicated, may hold values from -1.5 to 1.5
Outputs:
- block_out: bfloat16 [16, 8, 256, 384], P('batch', 'freq', 'tm')
- input_grad: bfloat16 [16, 8, 256, 384], P('batch', 'freq', 'tm')
- grad_mask_embed: float32 [384], replicated
- grad_ln1_gain: float32 [384], replicated
- grad_ln1_shift: float32 [384], replicated
- grad_w_qkv: float32 [384, 1152], replicated
- grad_bias_q: float32 [384], replicated
- grad_bias_v: float32 [384], replicated
- grad_w_out: float32 [384, 384], replicated
- grad_bias_out: float32 [384], replicated
- grad_ln2_gain: float32 [384], replicated
- grad_ln2_shift: float32 [384], replicated
- grad_w_up: float32 [384, 1536], replicated
- grad_bias_up: float32 [1536], replicated
- grad_w_down: float32 [1536, 384], replicated
- grad_bias_down: float32 [384], replicated
- soft_accuracy: float32 [16], P('batch')
All inputs are finite; a program needn't handle non-finite values. No bound on the sum of `patch_mask` on one device may be relied on, other than what follows from the above.
Results may differ from a plain program's by a relative error of at most 0.014.
Values may be sent and summed in bfloat16 or wider, within the bound.
A program may use at most 256 MiB of HBM per device.

v0:
```python
import jax
import jax.numpy as jnp
from jax import lax
from jax.sharding import PartitionSpec as P

D = 384
HEADS = 6
HEAD_DIM = 64
BLOCK_CLIPS = 4


def layer_norm(inputs, gain_vec, shift_vec):
    center = inputs - jnp.mean(inputs, axis=-1, keepdims=True)
    spread = jnp.mean(center * center, axis=-1, keepdims=True)
    return center * lax.rsqrt(spread + 1e-06) * gain_vec + shift_vec


def gelu_exact(inputs):
    return jax.nn.gelu(inputs, approximate=False)


def inner_rows(left_mat, right_mat):
    return lax.dot_general(
        left_mat, right_mat, (((0,), (0,)), ((), ())), preferred_element_type=jnp.float32
    )


def times_transpose(left_mat, right_mat):
    return lax.dot_general(
        left_mat, right_mat, (((1,), (1,)), ((), ())), preferred_element_type=jnp.float32
    )


def gather_keys(local):
    wider = lax.all_gather(local, "freq", axis=1, tiled=True)
    return lax.all_gather(wider, "tm", axis=2, tiled=True)


def gather_again(local):
    wider = lax.all_gather(local, "freq", axis=1, tiled=True)
    return lax.all_gather(wider, "tm", axis=2, tiled=True)


def split_heads(full_kv):
    blocks = full_kv.shape[0]
    flat_rows = full_kv.reshape(blocks, -1, 2 * D)
    key_rows = flat_rows[:, :, :D].reshape(blocks, -1, HEADS, HEAD_DIM)
    value_rows = flat_rows[:, :, D:].reshape(blocks, -1, HEADS, HEAD_DIM)
    return (key_rows, value_rows)


def masked_scores(queries, key_rows, lengths, full_kv):
    scores = jnp.einsum(
        "bqhd,bkhd->bhqk", queries, key_rows, preferred_element_type=jnp.float32
    ) * HEAD_DIM ** (-0.5)
    positions = lax.broadcasted_iota(
        jnp.int32, (full_kv.shape[0], full_kv.shape[1], full_kv.shape[2]), 2
    )
    usable = (positions < lengths[:, None, None]).reshape(full_kv.shape[0], -1)
    return jnp.where(usable[:, None, None, :], scores, -1000000000.0)


def attend_forward(queries, full_kv, lengths):
    key_rows, value_rows = split_heads(full_kv)
    scores = masked_scores(queries, key_rows, lengths, full_kv)
    row_max = jnp.max(scores, axis=-1, keepdims=True)
    raised = jnp.exp(scores - row_max)
    row_total = jnp.sum(raised, axis=-1, keepdims=True)
    attn_prob = (raised / row_total).astype(jnp.bfloat16)
    mixed = jnp.einsum("bhqk,bkhd->bqhd", attn_prob, value_rows, preferred_element_type=jnp.float32)
    return (mixed.astype(jnp.bfloat16), row_max + jnp.log(row_total))


def attend_backward(queries, full_kv, lengths, grad_mixed, log_total):
    key_rows, value_rows = split_heads(full_kv)
    scores = masked_scores(queries, key_rows, lengths, full_kv)
    attn_prob = jnp.exp(scores - log_total)
    grad_prob = jnp.einsum(
        "bqhd,bkhd->bhqk", grad_mixed, value_rows, preferred_element_type=jnp.float32
    )
    center = jnp.sum(attn_prob * grad_prob, axis=-1, keepdims=True)
    grad_scores = (attn_prob * (grad_prob - center)).astype(jnp.bfloat16)
    scale = HEAD_DIM ** (-0.5)
    grad_queries = (
        jnp.einsum("bhqk,bkhd->bqhd", grad_scores, key_rows, preferred_element_type=jnp.float32)
        * scale
    )
    grad_keys = (
        jnp.einsum("bhqk,bqhd->bkhd", grad_scores, queries, preferred_element_type=jnp.float32)
        * scale
    )
    grad_values = jnp.einsum(
        "bhqk,bqhd->bkhd",
        attn_prob.astype(jnp.bfloat16),
        grad_mixed,
        preferred_element_type=jnp.float32,
    )
    blocks = full_kv.shape[0]
    grad_full = jnp.concatenate(
        [grad_keys.reshape(blocks, -1, D), grad_values.reshape(blocks, -1, D)], axis=-1
    )
    grad_full = grad_full.reshape(full_kv.shape)
    own_part = lax.psum_scatter(
        grad_full.astype(jnp.bfloat16), "tm", scatter_dimension=2, tiled=True
    ).astype(jnp.float32)
    own_part = lax.psum_scatter(
        own_part.astype(jnp.bfloat16), "freq", scatter_dimension=1, tiled=True
    ).astype(jnp.float32)
    return (grad_queries.astype(jnp.bfloat16), own_part.astype(jnp.bfloat16))


def per_device(
    patches,
    patch_mask,
    clip_lengths,
    target_index,
    targets,
    out_grad,
    mask_embed,
    ln1_gain,
    ln1_shift,
    w_qkv,
    bias_q,
    bias_v,
    w_out,
    bias_out,
    ln2_gain,
    ln2_shift,
    w_up,
    bias_up,
    w_down,
    bias_down,
):
    clips, freq_rows, time_rows, width = patches.shape
    clip_rows = freq_rows * time_rows
    tokens = clips * clip_rows
    groups = clips // BLOCK_CLIPS
    masked = (patch_mask == 1)[..., None]
    flat_mask = masked.reshape(tokens, 1)
    start = jnp.where(masked, mask_embed.astype(jnp.float32), patches.astype(jnp.float32)).reshape(
        tokens, width
    )
    normed, first_back = jax.vjp(
        layer_norm, start, ln1_gain.astype(jnp.float32), ln1_shift.astype(jnp.float32)
    )
    normed_low = normed.astype(jnp.bfloat16)
    project = jnp.dot(normed_low, w_qkv, preferred_element_type=jnp.float32)
    queries = (project[:, :D] + bias_q.astype(jnp.float32)).astype(jnp.bfloat16)
    key_part = project[:, D : 2 * D]
    value_part = project[:, 2 * D :] + bias_v.astype(jnp.float32)
    local_kv = jnp.concatenate([key_part, value_part], axis=-1).astype(jnp.bfloat16)
    local_kv = local_kv.reshape(groups, BLOCK_CLIPS, freq_rows, time_rows, 2 * D)
    query_blocks = queries.reshape(groups, BLOCK_CLIPS, clip_rows, HEADS, HEAD_DIM)
    length_blocks = clip_lengths.reshape(groups, BLOCK_CLIPS)

    def forward_block(element):
        full_kv = gather_keys(element[1])
        return attend_forward(element[0], full_kv, element[2])

    mixed, log_total = lax.map(forward_block, (query_blocks, local_kv, length_blocks))
    mixed_rows = mixed.reshape(tokens, D)
    middle = (
        start
        + jnp.dot(mixed_rows, w_out, preferred_element_type=jnp.float32)
        + bias_out.astype(jnp.float32)
    )
    second, second_back = jax.vjp(
        layer_norm, middle, ln2_gain.astype(jnp.float32), ln2_shift.astype(jnp.float32)
    )
    second_low = second.astype(jnp.bfloat16)
    hidden_up = jnp.dot(second_low, w_up, preferred_element_type=jnp.float32) + bias_up.astype(
        jnp.float32
    )
    activated_f, gelu_back = jax.vjp(gelu_exact, hidden_up)
    activated = activated_f.astype(jnp.bfloat16)
    result = (
        middle
        + jnp.dot(activated, w_down, preferred_element_type=jnp.float32)
        + bias_down.astype(jnp.float32)
    )
    block_out = result.astype(jnp.bfloat16)
    grad_down = out_grad.reshape(tokens, width)
    grad_w_down = inner_rows(activated, grad_down)
    grad_bias_down = jnp.sum(grad_down.astype(jnp.float32), axis=0)
    grad_act = times_transpose(grad_down, w_down)
    grad_up = gelu_back(grad_act)[0].astype(jnp.bfloat16)
    grad_w_up = inner_rows(second_low, grad_up)
    grad_bias_up = jnp.sum(grad_up.astype(jnp.float32), axis=0)
    grad_second = times_transpose(grad_up, w_up)
    grad_middle_norm, grad_ln2_gain, grad_ln2_shift = second_back(grad_second)
    grad_middle = grad_down.astype(jnp.float32) + grad_middle_norm
    grad_branch = grad_middle.astype(jnp.bfloat16)
    grad_w_out = inner_rows(mixed_rows, grad_branch)
    grad_bias_out = jnp.sum(grad_branch.astype(jnp.float32), axis=0)
    grad_mixed = times_transpose(grad_branch, w_out).astype(jnp.bfloat16)
    grad_mixed = grad_mixed.reshape(groups, BLOCK_CLIPS, clip_rows, HEADS, HEAD_DIM)

    def backward_block(element):
        full_kv = gather_again(element[1])
        return attend_backward(element[0], full_kv, element[2], element[3], element[4])

    grad_queries, grad_kv = lax.map(
        backward_block, (query_blocks, local_kv, length_blocks, grad_mixed, log_total)
    )
    grad_query_rows = grad_queries.reshape(tokens, D)
    grad_kv_rows = grad_kv.reshape(tokens, 2 * D)
    grad_project = jnp.concatenate([grad_query_rows, grad_kv_rows], axis=-1)
    grad_w_qkv = inner_rows(normed_low, grad_project)
    grad_bias_q = jnp.sum(grad_query_rows.astype(jnp.float32), axis=0)
    grad_bias_v = jnp.sum(grad_kv_rows[:, D:].astype(jnp.float32), axis=0)
    grad_normed = times_transpose(grad_project, w_qkv)
    grad_start_norm, grad_ln1_gain, grad_ln1_shift = first_back(grad_normed)
    grad_start = grad_middle + grad_start_norm
    grad_mask_embed = jnp.sum(jnp.where(flat_mask, grad_start, 0.0), axis=0)
    input_grad = jnp.where(flat_mask, 0.0, grad_start).astype(jnp.bfloat16).reshape(patches.shape)
    summed = lax.psum(
        (
            grad_mask_embed,
            grad_ln1_gain,
            grad_ln1_shift,
            grad_w_qkv,
            grad_bias_q,
            grad_bias_v,
            grad_w_out,
            grad_bias_out,
            grad_ln2_gain,
            grad_ln2_shift,
            grad_w_up,
            grad_bias_up,
            grad_w_down,
            grad_bias_down,
        ),
        ("freq", "tm", "batch"),
    )
    out_rows = block_out.reshape(clips, clip_rows, width)
    logits = jnp.einsum("cqd,cnd->cqn", out_rows, targets, preferred_element_type=jnp.float32)
    logit_max = jnp.max(logits, axis=-1, keepdims=True)
    raised = jnp.exp(logits - logit_max)
    cand_prob = raised / jnp.sum(raised, axis=-1, keepdims=True)
    cand_ids = lax.broadcasted_iota(jnp.int32, cand_prob.shape, 2)
    picked = jnp.sum(
        jnp.where(cand_ids == target_index.reshape(clips, clip_rows)[..., None], cand_prob, 0.0),
        axis=-1,
    )
    positions = lax.axis_index("tm") * time_rows + lax.broadcasted_iota(
        jnp.int32, (clips, freq_rows, time_rows), 2
    )
    live_rows = (
        ((patch_mask == 1) & (positions < clip_lengths[:, None, None]))
        .reshape(clips, clip_rows)
        .astype(jnp.float32)
    )
    prob_sum, counted = lax.psum(
        (jnp.sum(picked * live_rows, axis=1), jnp.sum(live_rows, axis=1)), ("freq", "tm")
    )
    soft_accuracy = prob_sum / jnp.maximum(counted, 1.0)
    block_grid = block_out.reshape(patches.shape)
    return (
        block_grid,
        input_grad,
        summed[0],
        summed[1],
        summed[2],
        summed[3],
        summed[4],
        summed[5],
        summed[6],
        summed[7],
        summed[8],
        summed[9],
        summed[10],
        summed[11],
        summed[12],
        summed[13],
        soft_accuracy,
    )


def solution(mesh):
    in_specs = (
        P("batch", "freq", "tm", None),
        P("batch", "freq", "tm"),
        P("batch"),
        P("batch", "freq", "tm"),
        P("batch", None, None),
        P("batch", "freq", "tm", None),
        P(),
        P(),
        P(),
        P(),
        P(),
        P(),
        P(),
        P(),
        P(),
        P(),
        P(),
        P(),
        P(),
        P(),
    )
    out_specs = (
        P("batch", "freq", "tm", None),
        P("batch", "freq", "tm", None),
        P(),
        P(),
        P(),
        P(),
        P(),
        P(),
        P(),
        P(),
        P(),
        P(),
        P(),
        P(),
        P(),
        P(),
        P("batch"),
    )
    return jax.shard_map(
        per_device, mesh=mesh, in_specs=in_specs, out_specs=out_specs, check_vma=False
    )
```

profile of v0, /device:TPU:0, one launch (start us, length us, event | category | flops | bytes accessed | tf_op | source)
XLA Modules:
  0.0 1619.8 jit_solution(8345233267946131010)
XLA Ops:
  26.1 449.2 %while.24 = (s32[]{:T(128)}, bf16[2,4,128,6,64]{2,1,0,4,3:T(4,128)(2,1)}, f32[2,4,6,128,1]{3,2,1,4,0:T(8,128)}, bf16[2,4,4,32,768]{4,3,1,0,2:T(8,128)(2,1)S(1)},...) while((s32[]{:T(128)}, bf16[2,4,128,6,64]{2,1,0,4,3:T(4,128)(2,1)}, ...), condition=%wide.region_5.6_spmd, body=%wide.region_2.5_spmd.sunk | while | flops 1686311936 | bytes 244748528 | solution.py:160
  27.5 31.9 %all-gather.17.cloned.1.call-done = bf16[1,4,8,32,768]{4,3,1,0,2:T(8,128)(2,1)} async-done(((bf16[1,4,4,32,768]{4,3,1,0,2:T(8,128)(2,1)}), bf16[1,4,8,32,768]{4,3,1,0,2:T(8,128)(2,1)}) %all-gather.17.cloned.1.call-update) | async-done | bytes 1572880 | tf_op jit(solution)/shard_map/while/body/eval_jaxpr/all_gather | solution.py:35
  63.6 116.1 %all-gather.19.cloned.1.call-done = bf16[1,4,8,256,768]{4,2,1,0,3:T(8,128)(2,1)} async-done(((bf16[1,4,8,32,768]{4,2,1,0,3:T(8,128)(2,1)}), bf16[1,4,8,256,768]{4,2,1,0,3:T(8,128)(2,1)}) %all-gather.19.cloned.1.call-update) | async-done | bytes 12582928 | tf_op jit(solution)/shard_map/while/body/eval_jaxpr/all_gather | solution.py:36
  212.0 14.7 fusion.129
  253.9 27.5 %all-gather.17.cloned.1.call-done = bf16[1,4,8,32,768]{4,3,1,0,2:T(8,128)(2,1)} async-done(((bf16[1,4,4,32,768]{4,3,1,0,2:T(8,128)(2,1)}), bf16[1,4,8,32,768]{4,3,1,0,2:T(8,128)(2,1)}) %all-gather.17.cloned.1.call-update) | async-done | bytes 1572880 | tf_op jit(solution)/shard_map/while/body/eval_jaxpr/all_gather | solution.py:35
  285.6 116.1 %all-gather.19.cloned.1.call-done = bf16[1,4,8,256,768]{4,2,1,0,3:T(8,128)(2,1)} async-done(((bf16[1,4,8,32,768]{4,2,1,0,3:T(8,128)(2,1)}), bf16[1,4,8,256,768]{4,2,1,0,3:T(8,128)(2,1)}) %all-gather.19.cloned.1.call-update) | async-done | bytes 12582928 | tf_op jit(solution)/shard_map/while/body/eval_jaxpr/all_gather | solution.py:36
  434.0 14.7 fusion.129
  481.5 16.3 %multiply_convert_fusion.2 = (bf16[1024,1536]{1,0:T(8,128)(2,1)}, f32[1024,1536]{1,0:T(8,128)S(1)}, f32[1024,1536]{1,0:T(8,128)S(1)}) fusion(f32[1536]{0:T(1024)S(1)} %convert_element_type.124, bf16[384,1536]{1,0:T(8,128)(2,1)S(1)} %copy-done, f32[1024,384]{1,0:T(8,128)S(1)} %get-tuple-element.228, f32[384]{0:T(512)S(1)} %convert_element_type.122, ...), kind=kOutput, calls=%fused_computation.62 | convolution fusion | flops 1313734656 | bytes 18498560 | tf_op jit(solution)/shard_map/dot_general | solution.py:171
  515.6 912.0 %while.25 = (s32[]{:T(128)}, bf16[2,4,128,6,64]{2,4,3,1,0:T(8,128)(2,1)}, bf16[2,4,4,32,768]{4,3,2,1,0:T(8,128)(2,1)}, bf16[2,4,4,32,768]{4,3,1,0,2:T(8,128)(2,1...) while((s32[]{:T(128)}, ...), condition=%wide.region_14.15_spmd, body=%wide.region_10.14_spmd.sunk | while | flops 4155905024 | bytes 551883200 | solution.py:202
  521.1 27.0 %all-gather.21.cloned.1.call-done = bf16[1,4,8,32,768]{4,3,1,0,2:T(8,128)(2,1)} async-done(((bf16[1,4,4,32,768]{4,3,1,0,2:T(8,128)(2,1)}), bf16[1,4,8,32,768]{4,3,1,0,2:T(8,128)(2,1)}) %all-gather.21.cloned.1.call-update) | async-done | bytes 1572880 | tf_op jit(solution)/shard_map/while/body/eval_jaxpr/all_gather | solution.py:40
  553.2 115.2 %all-gather.23.cloned.1.call-done = bf16[1,4,8,256,768]{4,2,1,0,3:T(8,128)(2,1)} async-done(((bf16[1,4,8,32,768]{4,2,1,0,3:T(8,128)(2,1)}), bf16[1,4,8,256,768]{4,2,1,0,3:T(8,128)(2,1)}) %all-gather.23.cloned.1.call-update) | async-done | bytes 12582928 | tf_op jit(solution)/shard_map/while/body/eval_jaxpr/all_gather | solution.py:41
  700.5 14.6 fusion.142
  727.9 18.5 %multiply_reduce_fusion.8 = (f32[4,6,128]{2,1,0:T(8,128)S(1)}, f32[4,6,128,2048]{3,2,1,0:T(8,128)}) fusion(f32[4,6,128,2048]{3,2,1,0:T(8,128)} %fusion.142, f32[4,6,128]{2,1,0:T(8,128)S(1)} %copy-done.18, pred[4,2048]{1,0:T(4,128)(4,1)S(1)} %broadcast_compare_fusion.6, bf16[4,2048,6,64]{1,3,2,0:T(8,128)(2,1)} %bitcast.204, ...), kind=kOutput, calls=%fused_computation.22.clone.1 | convolution fusion | flops 836760576 | bytes 57049088 | tf_op jit(solution)/shard_map/while/body/eval_jaxpr/bqhd,bkhd->bhqk/dot_general | solution.py:78
  746.4 16.9 %multiply_convert_fusion.5 = bf16[4,6,128,2048]{3,2,1,0:T(8,128)(2,1)S(1)} fusion(f32[4,6,128,2048]{3,2,1,0:T(8,128)} %get-tuple-element.334, f32[4,6,128,2048]{3,2,1,0:T(8,128)} %fusion.142, f32[4,6,128]{2,1,0:T(8,128)S(1)} %get-tuple-element.335, f32[4,6,128]{2,1,0:T(8,128)S(1)} %copy-done.18, pred[4,2048]{1,0:T(4,128)(4,1)S(1)} %broadcast_compare_fusion.6), kind=kLoop, calls=%fused_computation.21.clone.1 | loop fusion | flops 37748736 | bytes 62947328 | tf_op jit(solution)/shard_map/while/body/eval_jaxpr/convert_element_type | solution.py:82
  811.4 127.6 %reduce-scatter.3.cloned.1.call-done = bf16[4,8,32,768]{3,1,0,2:T(8,128)(2,1)} async-done(((bf16[4,8,256,768]{3,1,0,2:T(8,128)(2,1)}), bf16[4,8,32,768]{3,1,0,2:T(8,128)(2,1)}) %reduce-scatter.3.cloned.1.call-update) | async-done | bytes 1572880 | tf_op jit(solution)/shard_map/while/body/eval_jaxpr/reduce_scatter | solution.py:103
  970.2 29.1 %all-gather.21.cloned.1.call-done = bf16[1,4,8,32,768]{4,3,1,0,2:T(8,128)(2,1)} async-done(((bf16[1,4,4,32,768]{4,3,1,0,2:T(8,128)(2,1)}), bf16[1,4,8,32,768]{4,3,1,0,2:T(8,128)(2,1)}) %all-gather.21.cloned.1.call-update) | async-done | bytes 1572880 | tf_op jit(solution)/shard_map/while/body/eval_jaxpr/all_gather | solution.py:40
  1004.5 115.2 %all-gather.23.cloned.1.call-done = bf16[1,4,8,256,768]{4,2,1,0,3:T(8,128)(2,1)} async-done(((bf16[1,4,8,32,768]{4,2,1,0,3:T(8,128)(2,1)}), bf16[1,4,8,256,768]{4,2,1,0,3:T(8,128)(2,1)}) %all-gather.23.cloned.1.call-update) | async-done | bytes 12582928 | tf_op jit(solution)/shard_map/while/body/eval_jaxpr/all_gather | solution.py:41
  1151.7 14.6 fusion.142
  1179.2 18.5 %multiply_reduce_fusion.8 = (f32[4,6,128]{2,1,0:T(8,128)S(1)}, f32[4,6,128,2048]{3,2,1,0:T(8,128)}) fusion(f32[4,6,128,2048]{3,2,1,0:T(8,128)} %fusion.142, f32[4,6,128]{2,1,0:T(8,128)S(1)} %copy-done.18, pred[4,2048]{1,0:T(4,128)(4,1)S(1)} %broadcast_compare_fusion.6, bf16[4,2048,6,64]{1,3,2,0:T(8,128)(2,1)} %bitcast.204, ...), kind=kOutput, calls=%fused_computation.22.clone.1 | convolution fusion | flops 836760576 | bytes 57049088 | tf_op jit(solution)/shard_map/while/body/eval_jaxpr/bqhd,bkhd->bhqk/dot_general | solution.py:78
  1197.7 16.9 %multiply_convert_fusion.5 = bf16[4,6,128,2048]{3,2,1,0:T(8,128)(2,1)S(1)} fusion(f32[4,6,128,2048]{3,2,1,0:T(8,128)} %get-tuple-element.334, f32[4,6,128,2048]{3,2,1,0:T(8,128)} %fusion.142, f32[4,6,128]{2,1,0:T(8,128)S(1)} %get-tuple-element.335, f32[4,6,128]{2,1,0:T(8,128)S(1)} %copy-done.18, pred[4,2048]{1,0:T(4,128)(4,1)S(1)} %broadcast_compare_fusion.6), kind=kLoop, calls=%fused_computation.21.clone.1 | loop fusion | flops 37748736 | bytes 62947328 | tf_op jit(solution)/shard_map/while/body/eval_jaxpr/convert_element_type | solution.py:82
  1262.7 127.5 %reduce-scatter.3.cloned.1.call-done = bf16[4,8,32,768]{3,1,0,2:T(8,128)(2,1)} async-done(((bf16[4,8,256,768]{3,1,0,2:T(8,128)(2,1)}), bf16[4,8,32,768]{3,1,0,2:T(8,128)(2,1)}) %reduce-scatter.3.cloned.1.call-update) | async-done | bytes 1572880 | tf_op jit(solution)/shard_map/while/body/eval_jaxpr/reduce_scatter | solution.py:103
  1446.8 33.9 %all-reduce.2 = (f32[8]{0:T(128)S(1)}, f32[8]{0:T(128)S(1)}) all-reduce(f32[8]{0:T(128)S(1)} %get-tuple-element.160, f32[8]{0:T(128)S(1)} %get-tuple-element.159), channel_id=1, replica_groups=mesh['freq'=2,'tm'=8,'batch'=2] {'freq','tm'}, use_global_device_ids=true, to_apply=%region_45.46 | all-reduce | flops 16 | bytes 128 | tf_op jit(solution)/shard_map/psum | solution.py:253
  1488.9 39.3 %all-reduce = (f32[384]{0:T(512)}, f32[384]{0:T(512)}, f32[384]{0:T(512)}, f32[384]{0:T(512)}, f32[384]{0:T(512)}, /*index=5*/f32[384]{0:T(512)}, f32[384]{0:T(512)}, f32[384]{0:T(512)}, f32[1536]{0:T(1024)}, f32[384]{0:T(512)}) all-reduce(f32[384]{0:T(512)S(1)} %get-tuple-element.223, ...), channel_id=1, replica_groups=mesh['freq'=2,'tm'=8,'batch'=2] {'freq','tm','batch'}, use_global_device_ids=true, to_apply=%region_18.19 | all-reduce | flops 4992 | bytes 39936 | tf_op jit(solution)/shard_map/psum | solution.py:216
  1528.8 75.7 %all-reduce.5.cloned.1.call-done = (f32[384,1152]{1,0:T(8,128)}, f32[384,384]{1,0:T(8,128)}, f32[384,1536]{1,0:T(8,128)}, f32[1536,384]{1,0:T(8,128)}) async-done(((f32[384,1152]{1,0:T(8,128)}, f32[384,384]{1,0:T(8,128)}, f32[384,1536]{1,0:T(8,128)}, f32[1536,384]{1,0:T(8,128)}), (f32[384,1152]{1,0:T(8,128)}, f32[384,384]{1,0:T(8,128)}, f32[384,1536]{1,0:T(8,128)}, ...) | async-done | bytes 7077904 | tf_op jit(solution)/shard_map/psum | solution.py:216
  (290 shorter events, 462.9 us)
Async XLA Ops:
  8.0 473.4 %copy-start = (bf16[384,1536]{1,0:T(8,128)(2,1)S(1)}, bf16[384,1536]{1,0:T(8,128)(2,1)}, u32[]{:S(2)}) copy-start(bf16[384,1536]{1,0:T(8,128)(2,1)} %param.40) | copy-start | bytes 3538948
  26.4 33.0 %all-gather.17.cloned.1.call-start = ((), (), s32[]{:S(2)}) async-start(), calls=%async_computation.3 | async-start | bytes 2359296 | tf_op jit(solution)/shard_map/while/body/eval_jaxpr/all_gather | solution.py:35
  27.5 152.3 %all-gather.19.cloned.1.call-start = ((), (), s32[]{:S(2)}) async-start(), calls=%async_computation.4 | async-start | bytes 14155776 | tf_op jit(solution)/shard_map/while/body/eval_jaxpr/all_gather | solution.py:36
  252.9 28.5 %all-gather.17.cloned.1.call-start = ((), (), s32[]{:S(2)}) async-start(), calls=%async_computation.3 | async-start | bytes 2359296 | tf_op jit(solution)/shard_map/while/body/eval_jaxpr/all_gather | solution.py:35
  253.8 147.8 %all-gather.19.cloned.1.call-start = ((), (), s32[]{:S(2)}) async-start(), calls=%async_computation.4 | async-start | bytes 14155776 | tf_op jit(solution)/shard_map/while/body/eval_jaxpr/all_gather | solution.py:36
  519.9 157.6 %copy-start.6 = (bf16[2,4,4,32,768]{4,3,1,0,2:T(8,128)(2,1)}, bf16[2,4,4,32,768]{4,3,1,0,2:T(8,128)(2,1)S(1)}, u32[]{:S(2)}) copy-start(bf16[2,4,4,32,768]{4,3,1,0,2:T(8,128)(2,1)S(1)} %get-tuple-element.378) | copy-start | bytes 4718596 | tf_op jit(solution)/shard_map/while
  519.9 180.6 %copy-start.4 = (bf16[2,4,128,6,64]{2,4,3,1,0:T(8,128)(2,1)}, bf16[2,4,128,6,64]{2,4,3,1,0:T(8,128)(2,1)S(1)}, u32[]{:S(2)}) copy-start(bf16[2,4,128,6,64]{2,4,3,1,0:T(8,128)(2,1)S(1)} %get-tuple-element.380) | copy-start | bytes 2359300 | tf_op jit(solution)/shard_map/while
  519.9 28.2 %all-gather.21.cloned.1.call-start = ((), (), s32[]{:S(2)}) async-start(), calls=%async_computation.5 | async-start | bytes 2359296 | tf_op jit(solution)/shard_map/while/body/eval_jaxpr/all_gather | solution.py:40
  521.0 147.4 %all-gather.23.cloned.1.call-start = ((), (), s32[]{:S(2)}) async-start(), calls=%async_computation.6 | async-start | bytes 14155776 | tf_op jit(solution)/shard_map/while/body/eval_jaxpr/all_gather | solution.py:41
  551.5 387.5 %reduce-scatter.3.cloned.1.call-start = ((), (), s32[]{:S(2)}) async-start(), calls=%async_computation.7 | async-start | bytes 14155776 | tf_op jit(solution)/shard_map/while/body/eval_jaxpr/reduce_scatter | solution.py:103
  811.4 155.6 %reduce-scatter.5.cloned.1.call-start = ((), (), s32[]{:S(2)}) async-start(), calls=%async_computation.8 | async-start | bytes 2359296 | tf_op jit(solution)/shard_map/while/body/eval_jaxpr/reduce_scatter | solution.py:106
  969.1 159.7 %copy-start.6 = (bf16[2,4,4,32,768]{4,3,1,0,2:T(8,128)(2,1)}, bf16[2,4,4,32,768]{4,3,1,0,2:T(8,128)(2,1)S(1)}, u32[]{:S(2)}) copy-start(bf16[2,4,4,32,768]{4,3,1,0,2:T(8,128)(2,1)S(1)} %get-tuple-element.378) | copy-start | bytes 4718596 | tf_op jit(solution)/shard_map/while
  969.1 182.7 %copy-start.4 = (bf16[2,4,128,6,64]{2,4,3,1,0:T(8,128)(2,1)}, bf16[2,4,128,6,64]{2,4,3,1,0:T(8,128)(2,1)S(1)}, u32[]{:S(2)}) copy-start(bf16[2,4,128,6,64]{2,4,3,1,0:T(8,128)(2,1)S(1)} %get-tuple-element.380) | copy-start | bytes 2359300 | tf_op jit(solution)/shard_map/while
  969.1 30.3 %all-gather.21.cloned.1.call-start = ((), (), s32[]{:S(2)}) async-start(), calls=%async_computation.5 | async-start | bytes 2359296 | tf_op jit(solution)/shard_map/while/body/eval_jaxpr/all_gather | solution.py:40
  970.2 149.5 %all-gather.23.cloned.1.call-start = ((), (), s32[]{:S(2)}) async-start(), calls=%async_computation.6 | async-start | bytes 14155776 | tf_op jit(solution)/shard_map/while/body/eval_jaxpr/all_gather | solution.py:41
  1002.8 387.5 %reduce-scatter.3.cloned.1.call-start = ((), (), s32[]{:S(2)}) async-start(), calls=%async_computation.7 | async-start | bytes 14155776 | tf_op jit(solution)/shard_map/while/body/eval_jaxpr/reduce_scatter | solution.py:103
  1262.7 155.6 %reduce-scatter.5.cloned.1.call-start = ((), (), s32[]{:S(2)}) async-start(), calls=%async_computation.8 | async-start | bytes 2359296 | tf_op jit(solution)/shard_map/while/body/eval_jaxpr/reduce_scatter | solution.py:106
  1427.7 176.8 %all-reduce.5.cloned.1.call-start = ((), (), s32[]{:S(2)}) async-start(), calls=%async_computation.2 | async-start | bytes 14155776 | tf_op jit(solution)/shard_map/psum | solution.py:216
  1438.8 42.0 %copy-start.19 = (bf16[2,4,128,6,64]{2,4,3,1,0:T(8,128)(2,1)S(1)}, bf16[2,4,128,6,64]{2,4,3,1,0:T(8,128)(2,1)}, u32[]{:S(2)}) copy-start(bf16[2,4,128,6,64]{2,4,3,1,0:T(8,128)(2,1)} %get-tuple-element.95) | copy-start | bytes 2359300
  1438.8 42.3 %copy-start.14 = (bf16[8,4,32,384]{3,2,1,0:T(8,128)(2,1)S(1)}, bf16[8,4,32,384]{3,2,1,0:T(8,128)(2,1)}, u32[]{:S(2)}) copy-start(bf16[8,4,32,384]{3,2,1,0:T(8,128)(2,1)} %param.29) | copy-start | bytes 2359300
  1438.8 43.8 %copy-start.9 = (f32[8,4,32,384]{3,2,1,0:T(8,128)S(1)}, f32[8,4,32,384]{3,2,1,0:T(8,128)}, u32[]{:S(2)}) copy-start(f32[8,4,32,384]{3,2,1,0:T(8,128)} %copy-done.8) | copy-start | bytes 4718596
  1438.8 43.8 %copy-start.33 = (f32[1024]{0:T(1024)S(1)}, f32[1024]{0:T(1024)}, u32[]{:S(2)}) copy-start(f32[1024]{0:T(1024)} %copy-done.32) | copy-start | bytes 12292
  1438.8 43.8 %copy-start.35 = (f32[1024]{0:T(1024)S(1)}, f32[1024]{0:T(1024)}, u32[]{:S(2)}) copy-start(f32[1024]{0:T(1024)} %copy-done.34) | copy-start | bytes 12292
  1438.8 43.8 %copy-start.37 = (f32[384]{0:T(512)S(1)}, f32[384]{0:T(512)}, u32[]{:S(2)}) copy-start(f32[384]{0:T(512)} %copy-done.36) | copy-start | bytes 4612
  (47 other events, 435.4 us)
Sparse Core Ops, SparseCore 0:
  29.5 29.8 all-gather.16
  63.0 116.7 all-gather.18
  255.9 25.4 all-gather.16
  284.9 116.7 all-gather.18
  522.6 25.4 all-gather.20
  551.6 116.7 all-gather.22
  811.5 127.4 reduce-scatter.2
  942.6 24.3 reduce-scatter.4
  972.1 27.2 all-gather.20
  1002.9 116.7 all-gather.22
  1262.8 127.4 reduce-scatter.2
  1393.8 24.4 reduce-scatter.4
Sparse Core Ops, SparseCore 1:
  1438.7 165.7 all-reduce.4
where the time goes:
time: 1630 us; the launch traced here: 1620 us
  waiting for transfers between devices  934 us (57%)
  local copies, waits for them, and re-layouts  257 us (16%)
  matrix products  230 us (14%)
  other arithmetic  96.1 us (6%)
  blocking collectives  73.2 us (4%)
  between operations  16.4 us (1%)
    reduce_scatter x2, waiting for transfers between devices, attend_backward(): lax.psum_scatter(grad_full.astype(jnp.bfloat16), 'tm', scatter_dimension=...  255 us
    all_gather x2, waiting for transfers between devices, gather_keys(): return lax.all_gather(wider, 'tm', axis=2, tiled=True)  232 us
    all_gather x2, waiting for transfers between devices, gather_again(): return lax.all_gather(wider, 'tm', axis=2, tiled=True)  230 us
    psum x1, waiting for transfers between devices, per_device(): lax.psum((grad_mask_embed, grad_ln1_gain, grad_ln1_shift, grad_w_qkv, gra...  75.7 us
    all_gather x2, waiting for transfers between devices, gather_keys(): wider = lax.all_gather(local, 'freq', axis=1, tiled=True)  59.4 us
    dot_general x4, matrix products, masked_scores(): jnp.einsum('bqhd,bkhd->bhqk', queries, key_rows, preferred_element_type=j...  58.5 us
    all_gather x2, waiting for transfers between devices, gather_again(): wider = lax.all_gather(local, 'freq', axis=1, tiled=True)  56.1 us
    slice x6, local copies, waits for them, and re-layouts, split_heads(): key_rows = flat_rows[:, :, :D].reshape(blocks, -1, HEADS, HEAD_DIM)  46.4 us
  transfers between devices with their start and end apart: 13, of which 13 were waited for; matrix products, arithmetic and copies ran while one was open for 3% of the time, Pallas kernels for 0%

commit v1 on v0

--- a/solution.py
+++ b/solution.py
@@ -214,23 +214,26 @@
     grad_mask_embed = jnp.sum(jnp.where(flat_mask, grad_start, 0.0), axis=0)
     input_grad = jnp.where(flat_mask, 0.0, grad_start).astype(jnp.bfloat16).reshape(patches.shape)
     summed = lax.psum(
-        (
-            grad_mask_embed,
-            grad_ln1_gain,
-            grad_ln1_shift,
-            grad_w_qkv,
-            grad_bias_q,
-            grad_bias_v,
-            grad_w_out,
-            grad_bias_out,
-            grad_ln2_gain,
-            grad_ln2_shift,
-            grad_w_up,
-            grad_bias_up,
-            grad_w_down,
-            grad_bias_down,
+        lax.psum(
+            (
+                grad_mask_embed,
+                grad_ln1_gain,
+                grad_ln1_shift,
+                grad_w_qkv,
+                grad_bias_q,
+                grad_bias_v,
+                grad_w_out,
+                grad_bias_out,
+                grad_ln2_gain,
+                grad_ln2_shift,
+                grad_w_up,
+                grad_bias_up,
+                grad_w_down,
+                grad_bias_down,
+            ),
+            ("tm", "batch"),
         ),
-        ("freq", "tm", "batch"),
+        "freq",
     )
     out_rows = block_out.reshape(clips, clip_rows, width)
     logits = jnp.einsum("cqd,cnd->cqn", out_rows, targets, preferred_element_type=jnp.float32)

time: 1630 us -> 1790 us (1.098)
  waiting for transfers between devices: 934 us -> 1070 us
  blocking collectives: 73.2 us -> 101 us
    psum x1, waiting for transfers between devices: 75.7 us -> 152 us  [per_device(): lax.psum((grad_mask_embed, grad_ln1_gain, grad_ln1_shift, grad_w_qkv, gra...]
    psum x0 -> x1, waiting for transfers between devices: none -> 57.2 us  [per_device(): lax.psum(lax.psum((grad_mask_embed, grad_ln1_gain, grad_ln1_shift, grad_w...]
    psum x1, blocking collectives: 39.3 us -> 59 us  [per_device(): lax.psum((grad_mask_embed, grad_ln1_gain, grad_ln1_shift, grad_w_qkv, gra...]
  transfers between devices with their start and end apart: 13 -> 14, of which waited for: 13 -> 14; matrix products, arithmetic and copies ran while one was open for 3% -> 3% of each run, Pallas kernels for 0% -> 0%
where the time goes in v1:
time: 1790 us; the launch traced here: 1780 us
  waiting for transfers between devices  1070 us (60%)
  local copies, waits for them, and re-layouts  257 us (14%)
  matrix products  229 us (13%)
  blocking collectives  101 us (6%)
  other arithmetic  96.1 us (5%)
    reduce_scatter x2, waiting for transfers between devices, attend_backward(): lax.psum_scatter(grad_full.astype(jnp.bfloat16), 'tm', scatter_dimension=...  255 us
    all_gather x2, waiting for transfers between devices, gather_keys(): return lax.all_gather(wider, 'tm', axis=2, tiled=True)  232 us
    all_gather x2, waiting for transfers between devices, gather_again(): return lax.all_gather(wider, 'tm', axis=2, tiled=True)  230 us
    psum x1, waiting for transfers between devices, per_device(): lax.psum((grad_mask_embed, grad_ln1_gain, grad_ln1_shift, grad_w_qkv, gra...  152 us
    all_gather x2, waiting for transfers between devices, gather_keys(): wider = lax.all_gather(local, 'freq', axis=1, tiled=True)  59.4 us
    psum x1, blocking collectives, per_device(): lax.psum((grad_mask_embed, grad_ln1_gain, grad_ln1_shift, grad_w_qkv, gra...  59 us
    dot_general x4, matrix products, masked_scores(): jnp.einsum('bqhd,bkhd->bhqk', queries, key_rows, preferred_element_type=j...  58.5 us
    psum x1, waiting for transfers between devices, per_device(): lax.psum(lax.psum((grad_mask_embed, grad_ln1_gain, grad_ln1_shift, grad_w...  57.2 us
  transfers between devices with their start and end apart: 14, of which 14 were waited for; matrix products, arithmetic and copies ran while one was open for 3% of the time, Pallas kernels for 0%

profile of v1, /device:TPU:0, one launch (start us, length us, event | category | flops | bytes accessed | tf_op | source)
XLA Modules:
  0.0 1780.0 jit_solution(17715394955312094295)
XLA Ops:
  26.1 449.2 %while.24 = (s32[]{:T(128)}, bf16[2,4,128,6,64]{2,1,0,4,3:T(4,128)(2,1)}, f32[2,4,6,128,1]{3,2,1,4,0:T(8,128)}, bf16[2,4,4,32,768]{4,3,1,0,2:T(8,128)(2,1)S(1)},...) while((s32[]{:T(128)}, bf16[2,4,128,6,64]{2,1,0,4,3:T(4,128)(2,1)}, ...), condition=%wide.region_5.6_spmd, body=%wide.region_2.5_spmd.sunk | while | flops 1686311936 | bytes 244748528 | solution.py:160
  27.5 31.9 %all-gather.17.cloned.1.call-done = bf16[1,4,8,32,768]{4,3,1,0,2:T(8,128)(2,1)} async-done(((bf16[1,4,4,32,768]{4,3,1,0,2:T(8,128)(2,1)}), bf16[1,4,8,32,768]{4,3,1,0,2:T(8,128)(2,1)}) %all-gather.17.cloned.1.call-update) | async-done | bytes 1572880 | tf_op jit(solution)/shard_map/while/body/eval_jaxpr/all_gather | solution.py:35
  63.6 116.1 %all-gather.19.cloned.1.call-done = bf16[1,4,8,256,768]{4,2,1,0,3:T(8,128)(2,1)} async-done(((bf16[1,4,8,32,768]{4,2,1,0,3:T(8,128)(2,1)}), bf16[1,4,8,256,768]{4,2,1,0,3:T(8,128)(2,1)}) %all-gather.19.cloned.1.call-update) | async-done | bytes 12582928 | tf_op jit(solution)/shard_map/while/body/eval_jaxpr/all_gather | solution.py:36
  212.0 14.7 fusion.129
  253.9 27.5 %all-gather.17.cloned.1.call-done = bf16[1,4,8,32,768]{4,3,1,0,2:T(8,128)(2,1)} async-done(((bf16[1,4,4,32,768]{4,3,1,0,2:T(8,128)(2,1)}), bf16[1,4,8,32,768]{4,3,1,0,2:T(8,128)(2,1)}) %all-gather.17.cloned.1.call-update) | async-done | bytes 1572880 | tf_op jit(solution)/shard_map/while/body/eval_jaxpr/all_gather | solution.py:35
  285.6 116.1 %all-gather.19.cloned.1.call-done = bf16[1,4,8,256,768]{4,2,1,0,3:T(8,128)(2,1)} async-done(((bf16[1,4,8,32,768]{4,2,1,0,3:T(8,128)(2,1)}), bf16[1,4,8,256,768]{4,2,1,0,3:T(8,128)(2,1)}) %all-gather.19.cloned.1.call-update) | async-done | bytes 12582928 | tf_op jit(solution)/shard_map/while/body/eval_jaxpr/all_gather | solution.py:36
  434.0 14.7 fusion.129
  481.5 16.3 multiply_convert_fusion.2
  515.6 911.9 %while.25 = (s32[]{:T(128)}, bf16[2,4,128,6,64]{2,4,3,1,0:T(8,128)(2,1)}, bf16[2,4,4,32,768]{4,3,2,1,0:T(8,128)(2,1)}, bf16[2,4,4,32,768]{4,3,1,0,2:T(8,128)(2,1...) while((s32[]{:T(128)}, ...), condition=%wide.region_14.15_spmd, body=%wide.region_10.14_spmd.sunk | while | flops 4155905024 | bytes 551883200 | solution.py:202
  521.1 27.0 %all-gather.21.cloned.1.call-done = bf16[1,4,8,32,768]{4,3,1,0,2:T(8,128)(2,1)} async-done(((bf16[1,4,4,32,768]{4,3,1,0,2:T(8,128)(2,1)}), bf16[1,4,8,32,768]{4,3,1,0,2:T(8,128)(2,1)}) %all-gather.21.cloned.1.call-update) | async-done | bytes 1572880 | tf_op jit(solution)/shard_map/while/body/eval_jaxpr/all_gather | solution.py:40
  553.2 115.2 %all-gather.23.cloned.1.call-done = bf16[1,4,8,256,768]{4,2,1,0,3:T(8,128)(2,1)} async-done(((bf16[1,4,8,32,768]{4,2,1,0,3:T(8,128)(2,1)}), bf16[1,4,8,256,768]{4,2,1,0,3:T(8,128)(2,1)}) %all-gather.23.cloned.1.call-update) | async-done | bytes 12582928 | tf_op jit(solution)/shard_map/while/body/eval_jaxpr/all_gather | solution.py:41
  727.9 18.5 %multiply_reduce_fusion.8 = (f32[4,6,128]{2,1,0:T(8,128)S(1)}, f32[4,6,128,2048]{3,2,1,0:T(8,128)}) fusion(f32[4,6,128,2048]{3,2,1,0:T(8,128)} %fusion.142, f32[4,6,128]{2,1,0:T(8,128)S(1)} %copy-done.18, pred[4,2048]{1,0:T(4,128)(4,1)S(1)} %broadcast_compare_fusion.6, bf16[4,2048,6,64]{1,3,2,0:T(8,128)(2,1)} %bitcast.204, ...), kind=kOutput, calls=%fused_computation.22.clone.1 | convolution fusion | flops 836760576 | bytes 57049088 | tf_op jit(solution)/shard_map/while/body/eval_jaxpr/bqhd,bkhd->bhqk/dot_general | solution.py:78
  746.4 16.9 multiply_convert_fusion.5
  811.4 127.6 %reduce-scatter.3.cloned.1.call-done = bf16[4,8,32,768]{3,1,0,2:T(8,128)(2,1)} async-done(((bf16[4,8,256,768]{3,1,0,2:T(8,128)(2,1)}), bf16[4,8,32,768]{3,1,0,2:T(8,128)(2,1)}) %reduce-scatter.3.cloned.1.call-update) | async-done | bytes 1572880 | tf_op jit(solution)/shard_map/while/body/eval_jaxpr/reduce_scatter | solution.py:103
  970.3 29.1 %all-gather.21.cloned.1.call-done = bf16[1,4,8,32,768]{4,3,1,0,2:T(8,128)(2,1)} async-done(((bf16[1,4,4,32,768]{4,3,1,0,2:T(8,128)(2,1)}), bf16[1,4,8,32,768]{4,3,1,0,2:T(8,128)(2,1)}) %all-gather.21.cloned.1.call-update) | async-done | bytes 1572880 | tf_op jit(solution)/shard_map/while/body/eval_jaxpr/all_gather | solution.py:40
  1004.5 115.2 %all-gather.23.cloned.1.call-done = bf16[1,4,8,256,768]{4,2,1,0,3:T(8,128)(2,1)} async-done(((bf16[1,4,8,32,768]{4,2,1,0,3:T(8,128)(2,1)}), bf16[1,4,8,256,768]{4,2,1,0,3:T(8,128)(2,1)}) %all-gather.23.cloned.1.call-update) | async-done | bytes 12582928 | tf_op jit(solution)/shard_map/while/body/eval_jaxpr/all_gather | solution.py:41
  1151.7 14.6 fusion.142
  1179.2 18.5 %multiply_reduce_fusion.8 = (f32[4,6,128]{2,1,0:T(8,128)S(1)}, f32[4,6,128,2048]{3,2,1,0:T(8,128)}) fusion(f32[4,6,128,2048]{3,2,1,0:T(8,128)} %fusion.142, f32[4,6,128]{2,1,0:T(8,128)S(1)} %copy-done.18, pred[4,2048]{1,0:T(4,128)(4,1)S(1)} %broadcast_compare_fusion.6, bf16[4,2048,6,64]{1,3,2,0:T(8,128)(2,1)} %bitcast.204, ...), kind=kOutput, calls=%fused_computation.22.clone.1 | convolution fusion | flops 836760576 | bytes 57049088 | tf_op jit(solution)/shard_map/while/body/eval_jaxpr/bqhd,bkhd->bhqk/dot_general | solution.py:78
  1197.7 16.9 multiply_convert_fusion.5
  1262.7 127.5 %reduce-scatter.3.cloned.1.call-done = bf16[4,8,32,768]{3,1,0,2:T(8,128)(2,1)} async-done(((bf16[4,8,256,768]{3,1,0,2:T(8,128)(2,1)}), bf16[4,8,32,768]{3,1,0,2:T(8,128)(2,1)}) %reduce-scatter.3.cloned.1.call-update) | async-done | bytes 1572880 | tf_op jit(solution)/shard_map/while/body/eval_jaxpr/reduce_scatter | solution.py:103
  1438.6 151.5 %all-reduce.8.cloned.1.call-done = (f32[384,1152]{1,0:T(8,128)}, f32[384,384]{1,0:T(8,128)}, f32[384,1536]{1,0:T(8,128)}, f32[1536,384]{1,0:T(8,128)}) async-done(((f32[384,1152]{1,0:T(8,128)}, f32[384,384]{1,0:T(8,128)}, f32[384,1536]{1,0:T(8,128)}, f32[1536,384]{1,0:T(8,128)}), (f32[384,1152]{1,0:T(8,128)}, f32[384,384]{1,0:T(8,128)}, f32[384,1536]{1,0:T(8,128)}, ...) | async-done | bytes 7077904 | tf_op jit(solution)/shard_map/psum | solution.py:217
  1598.1 33.1 %all-reduce.2 = (f32[8]{0:T(128)S(1)}, f32[8]{0:T(128)S(1)}) all-reduce(f32[8]{0:T(128)S(1)} %get-tuple-element.160, f32[8]{0:T(128)S(1)} %get-tuple-element.159), channel_id=1, replica_groups=mesh['freq'=2,'tm'=8,'batch'=2] {'freq','tm'}, use_global_device_ids=true, to_apply=%region_59.60 | all-reduce | flops 16 | bytes 128 | tf_op jit(solution)/shard_map/psum | solution.py:256
  1639.4 59.0 %all-reduce = (f32[384]{0:T(512)S(1)}, f32[384]{0:T(512)S(1)}, f32[384]{0:T(512)S(1)}, f32[384]{0:T(512)S(1)}, f32[384]{0:T(512)S(1)}, /*index=5*/f32[384]{0:T(5...) all-reduce(f32[384]{0:T(512)S(1)} %get-tuple-element.237, ...), channel_id=1, replica_groups=mesh['freq'=2,'tm'=8,'batch'=2] {'tm','batch'}, use_global_device_ids=true, to_apply=%region_18.19 | all-reduce | flops 4992 | bytes 39936 | tf_op jit(solution)/shard_map/psum | solution.py:217
  1707.5 57.2 %all-reduce.10.cloned.1.call-done = (f32[384,1152]{1,0:T(8,128)}, f32[384,384]{1,0:T(8,128)}, f32[384,1536]{1,0:T(8,128)}, f32[1536,384]{1,0:T(8,128)}) async-done(((f32[384,1152]{1,0:T(8,128)}, f32[384,384]{1,0:T(8,128)}, f32[384,1536]{1,0:T(8,128)}, f32[1536,384]{1,0:T(8,128)}), (f32[384,1152]{1,0:T(8,128)}, f32[384,384]{1,0:T(8,128)}, f32[384,1536]{1,0:T(8,128)}, ...) | async-done | bytes 7077904 | tf_op jit(solution)/shard_map/psum | solution.py:216
  (294 shorter events, 485.9 us)
Async XLA Ops:
  8.0 473.4 %copy-start = (bf16[384,1536]{1,0:T(8,128)(2,1)S(1)}, bf16[384,1536]{1,0:T(8,128)(2,1)}, u32[]{:S(2)}) copy-start(bf16[384,1536]{1,0:T(8,128)(2,1)} %param.40) | copy-start | bytes 3538948
  26.4 33.0 %all-gather.17.cloned.1.call-start = ((), (), s32[]{:S(2)}) async-start(), calls=%async_computation.4 | async-start | bytes 2359296 | tf_op jit(solution)/shard_map/while/body/eval_jaxpr/all_gather | solution.py:35
  27.5 152.3 %all-gather.19.cloned.1.call-start = ((), (), s32[]{:S(2)}) async-start(), calls=%async_computation.5 | async-start | bytes 14155776 | tf_op jit(solution)/shard_map/while/body/eval_jaxpr/all_gather | solution.py:36
  252.9 28.5 %all-gather.17.cloned.1.call-start = ((), (), s32[]{:S(2)}) async-start(), calls=%async_computation.4 | async-start | bytes 2359296 | tf_op jit(solution)/shard_map/while/body/eval_jaxpr/all_gather | solution.py:35
  253.8 147.8 %all-gather.19.cloned.1.call-start = ((), (), s32[]{:S(2)}) async-start(), calls=%async_computation.5 | async-start | bytes 14155776 | tf_op jit(solution)/shard_map/while/body/eval_jaxpr/all_gather | solution.py:36
  519.9 157.6 %copy-start.6 = (bf16[2,4,4,32,768]{4,3,1,0,2:T(8,128)(2,1)}, bf16[2,4,4,32,768]{4,3,1,0,2:T(8,128)(2,1)S(1)}, u32[]{:S(2)}) copy-start(bf16[2,4,4,32,768]{4,3,1,0,2:T(8,128)(2,1)S(1)} %get-tuple-element.392) | copy-start | bytes 4718596 | tf_op jit(solution)/shard_map/while
  519.9 180.6 %copy-start.4 = (bf16[2,4,128,6,64]{2,4,3,1,0:T(8,128)(2,1)}, bf16[2,4,128,6,64]{2,4,3,1,0:T(8,128)(2,1)S(1)}, u32[]{:S(2)}) copy-start(bf16[2,4,128,6,64]{2,4,3,1,0:T(8,128)(2,1)S(1)} %get-tuple-element.394) | copy-start | bytes 2359300 | tf_op jit(solution)/shard_map/while
  519.9 28.2 %all-gather.21.cloned.1.call-start = ((), (), s32[]{:S(2)}) async-start(), calls=%async_computation.6 | async-start | bytes 2359296 | tf_op jit(solution)/shard_map/while/body/eval_jaxpr/all_gather | solution.py:40
  521.0 147.4 %all-gather.23.cloned.1.call-start = ((), (), s32[]{:S(2)}) async-start(), calls=%async_computation.7 | async-start | bytes 14155776 | tf_op jit(solution)/shard_map/while/body/eval_jaxpr/all_gather | solution.py:41
  551.5 387.5 %reduce-scatter.3.cloned.1.call-start = ((), (), s32[]{:S(2)}) async-start(), calls=%async_computation.8 | async-start | bytes 14155776 | tf_op jit(solution)/shard_map/while/body/eval_jaxpr/reduce_scatter | solution.py:103
  811.4 155.6 %reduce-scatter.5.cloned.1.call-start = ((), (), s32[]{:S(2)}) async-start(), calls=%async_computation.9 | async-start | bytes 2359296 | tf_op jit(solution)/shard_map/while/body/eval_jaxpr/reduce_scatter | solution.py:106
  969.1 159.7 %copy-start.6 = (bf16[2,4,4,32,768]{4,3,1,0,2:T(8,128)(2,1)}, bf16[2,4,4,32,768]{4,3,1,0,2:T(8,128)(2,1)S(1)}, u32[]{:S(2)}) copy-start(bf16[2,4,4,32,768]{4,3,1,0,2:T(8,128)(2,1)S(1)} %get-tuple-element.392) | copy-start | bytes 4718596 | tf_op jit(solution)/shard_map/while
  969.1 182.7 %copy-start.4 = (bf16[2,4,128,6,64]{2,4,3,1,0:T(8,128)(2,1)}, bf16[2,4,128,6,64]{2,4,3,1,0:T(8,128)(2,1)S(1)}, u32[]{:S(2)}) copy-start(bf16[2,4,128,6,64]{2,4,3,1,0:T(8,128)(2,1)S(1)} %get-tuple-element.394) | copy-start | bytes 2359300 | tf_op jit(solution)/shard_map/while
  969.1 30.3 %all-gather.21.cloned.1.call-start = ((), (), s32[]{:S(2)}) async-start(), calls=%async_computation.6 | async-start | bytes 2359296 | tf_op jit(solution)/shard_map/while/body/eval_jaxpr/all_gather | solution.py:40
  970.2 149.5 %all-gather.23.cloned.1.call-start = ((), (), s32[]{:S(2)}) async-start(), calls=%async_computation.7 | async-start | bytes 14155776 | tf_op jit(solution)/shard_map/while/body/eval_jaxpr/all_gather | solution.py:41
  1002.8 387.5 %reduce-scatter.3.cloned.1.call-start = ((), (), s32[]{:S(2)}) async-start(), calls=%async_computation.8 | async-start | bytes 14155776 | tf_op jit(solution)/shard_map/while/body/eval_jaxpr/reduce_scatter | solution.py:103
  1262.7 155.6 %reduce-scatter.5.cloned.1.call-start = ((), (), s32[]{:S(2)}) async-start(), calls=%async_computation.9 | async-start | bytes 2359296 | tf_op jit(solution)/shard_map/while/body/eval_jaxpr/reduce_scatter | solution.py:106
  1427.6 162.5 %all-reduce.8.cloned.1.call-start = ((), (), s32[]{:S(2)}) async-start(), calls=%async_computation.2 | async-start | bytes 14155776 | tf_op jit(solution)/shard_map/psum | solution.py:217
  1438.5 151.6 %copy-start.46 = (bf16[384]{0:T(512)(128)(2,1)S(1)}, bf16[384]{0:T(512)(128)(2,1)}, u32[]{:S(2)}) copy-start(bf16[384]{0:T(512)(128)(2,1)} %param.43) | copy-start | bytes 2308
  1438.5 151.6 %copy-start.38 = (s32[8,4,32]{2,1,0:T(4,128)S(1)}, s32[8,4,32]{2,1,0:T(4,128)}, u32[]{:S(2)}) copy-start(s32[8,4,32]{2,1,0:T(4,128)} %param.27) | copy-start | bytes 12292
  1438.5 326.2 %all-reduce.10.cloned.1.call-start = ((), (), s32[]{:S(2)}) async-start(), calls=%async_computation.3 | async-start | bytes 14155776 | tf_op jit(solution)/shard_map/psum | solution.py:216
  1590.3 42.7 %copy-start.9 = (f32[8,4,32,384]{3,2,1,0:T(8,128)S(1)}, f32[8,4,32,384]{3,2,1,0:T(8,128)}, u32[]{:S(2)}) copy-start(f32[8,4,32,384]{3,2,1,0:T(8,128)} %copy-done.8) | copy-start | bytes 4718596
  1590.3 42.7 %copy-start.33 = (f32[1024]{0:T(1024)S(1)}, f32[1024]{0:T(1024)}, u32[]{:S(2)}) copy-start(f32[1024]{0:T(1024)} %copy-done.32) | copy-start | bytes 12292
  1590.3 42.7 %copy-start.35 = (f32[1024]{0:T(1024)S(1)}, f32[1024]{0:T(1024)}, u32[]{:S(2)}) copy-start(f32[1024]{0:T(1024)} %copy-done.34) | copy-start | bytes 12292
  (48 other events, 553.8 us)
Sparse Core Ops, SparseCore 0:
  29.5 29.8 all-gather.16
  63.0 116.7 all-gather.18
  255.9 25.4 all-gather.16
  284.9 116.7 all-gather.18
  522.6 25.4 all-gather.20
  551.6 116.7 all-gather.22
  811.5 127.4 reduce-scatter.2
  942.6 24.3 reduce-scatter.4
  972.1 27.2 all-gather.20
  1002.9 116.7 all-gather.22
  1262.8 127.4 reduce-scatter.2
  1393.8 24.4 reduce-scatter.4
Sparse Core Ops, SparseCore 1:
  1438.6 151.4 all-reduce.7
  1592.6 172.1 all-reduce.9
